TPU v7x, 32 devices: a whole 2x2x4 slice. The times are simulated.
32 devices in a mesh: seq: 8 (over z, x), batch: 4 (over y, core).
Axes of the slice: x: 2, y: 2, z: 4, core: 2. Of those that a mesh axis runs over, the one named last changes fastest.
Arguments:
- inputs: bfloat16 [4, 1024, 768], P('batch', 'seq'), may hold values from -6 to 6
- cotangent: bfloat16 [4, 1024, 768], P('batch', 'seq'), may hold values from -6 to 6
- doc_lengths: int32 [4, 9], P('batch'), may hold values from 1 to 896, as said below
- gain_one: float32 [768], replicated, may hold values from 0.5 to 1.5
- shift_one: float32 [768], replicated, may hold values from -2 to 2
- qkv_weight: bfloat16 [768, 2304], replicated, may hold values from -0.21875 to 0.21875
- qkv_bias: float32 [2304], replicated, may hold values from -2 to 2
- proj_weight: bfloat16 [768, 768], replicated, may hold values from -6 to 6
- proj_bias: float32 [768], replicated, may hold values from -2 to 2
- gain_two: float32 [768], replicated, may hold values from 0.5 to 1.5
- shift_two: float32 [768], replicated, may hold values from -2 to 2
- up_weight: bfloat16 [768, 3072], replicated, may hold values from -0.21875 to 0.21875
- up_bias: float32 [3072], replicated, may hold values from -2 to 2
- down_weight: bfloat16 [3072, 768], replicated, may hold values from -0.109375 to 0.109375
- down_bias: float32 [768], replicated, may hold values from -2 to 2
Outputs:
- layer_out: bfloat16 [4, 1024, 768], P('batch', 'seq')
- input_grad: bfloat16 [4, 1024, 768], P('batch', 'seq')
- grad_gain_one: float32 [768], replicated
- grad_shift_one: float32 [768], replicated
- grad_qkv_weight: float32 [768, 2304], replicated
- grad_qkv_bias: float32 [2304], replicated
- grad_proj_weight: float32 [768, 768], replicated
- grad_proj_bias: float32 [768], replicated
- grad_gain_two: float32 [768], replicated
- grad_shift_two: float32 [768], replicated
- grad_up_weight: float32 [768, 3072], replicated
- grad_up_bias: float32 [3072], replicated
- grad_down_weight: float32 [3072, 768], replicated
- grad_down_bias: float32 [768], replicated
Inputs may be any that keep to these rules, and one draw needn't show every extreme that they name: `doc_lengths`: each row lists in order the lengths of the 9 documents packed into one stream: 8 short ones that hold 128 tokens together, and one of exactly 896 tokens with at least one short document before it and one after it.
All inputs are finite; a program needn't handle non-finite values.
Results may differ from a plain program's by a relative error of at most 0.018.
Values may be sent and summed in bfloat16 or wider, within the bound.
A program may use at most 256 MiB of HBM per device.

v0:
```python
import functools
import math

import jax
import jax.numpy as jnp
from jax import lax
from jax.experimental import pallas as pl
from jax.experimental.pallas import tpu as pltpu
from jax.sharding import PartitionSpec as P

HEADS = 12
HD = 64


norm_eps = 1e-05
masked_low = -1e30


MESH_ID = pl.DeviceIdType.MESH
TILE = 16
LANES = 128
FF_TILE = 768
ITEM = 256
KINDS = "11133300404055354145"
GROUPS = 5
PACE = 8
UNROLL = 2
FAR = ("down", "up")
TURNED = 2
K2_LIMIT = 45
KEPT = (0,)
WIDEN = 128 * 2304
SMALL_ROWS = ((11, 1), (12, 1), (8, 3), (3, 1), (0, 1), (1, 1), (4, 4), (2, 1))
SCHEDULE = (
    -1, 12, -2, 13, 12, 0, 6, 13, -3, 12, 6, 0, 1, 2, 9, 10, 11, 13, 6, 8, 7, -4, 6, 11, 10, 4, 12, 0, 3, 2, 5, 6, 7,
    -5, 2, 9, 1, 13, 12, 11, -6, 9, 2, 1, 4, 6, 8, 3, 10, -7, 18, 4, 19, 6, 14, 5, 3, 8, 16, 1, 7, 10, 9, 6, 19, 7, 4,
    15, 18, 12, 17, 5, 3, 20, 15, 11, 0, 7, 9, 20, 14, 5, 18, 3, 2, 16, 7, 15, 4, 9, 13, 3, 19, 16, 10, 7, 5, 18, 5,
    6, 17, 8, 17, 12, 14, 15, 2, 1, 19, 7, 16, 13, 10, 15, 14, 20, 18, 3, 8, 14, 16, 0, 18, 17, 2, 7, 10, 1, 15, 11,
    9, 2, 14, 13, 16, 19, 17, 5, 9, 18, 1, 3, 0, 2, 4, 19, 8, 17, 7, 14, 18, 11, 15, 10, 20, 5, 0, 14, 19, 9, 4, 3,
    18, 16, 15, 14, 19, 13, 16, 5, 4, 1, 10, 1, 8, 11, 3, 16, 15, 11, 8, 12, 0, 5, 17, 18, 15, 8, 9, 19, 10, 12, 14,
    20, 17, 11, 4, 12, 13, 16, 0, 14, 17, 20, 15, 8, 13, 19, 12, 6, 4, 17, 16, 0, 17, 18, 11, 19, 13, 1, 2,
)


class Place:
    def __init__(self):
        self.seq = lax.axis_index("seq")
        self.batch = lax.axis_index("batch")
        self.level = self.seq // 2
        self.levels = lax.axis_size("seq") // 2

    def bit(self, axis):
        name, k = axis
        return ((self.seq if name == "seq" else self.batch) // (1 << k)) % 2

    def partner(self, axis):
        name, k = axis
        step = (1 << k) * (1 - 2 * self.bit(axis))
        if name == "seq":
            return (self.seq + step, self.batch)
        return (self.seq, self.batch + step)


CORE = ("batch", 0)
ACROSS = ("batch", 1)
LEVELS = ("seq", None)


def seq_axes(peers):
    return [("seq", k) for k in range((peers - 1).bit_length())]


def axis_orders():
    x, y, z = ("seq", 0), ACROSS, LEVELS
    return [[x, y, z], [y, z, x], [z, x, y], [y, x, z], [x, z, y], [z, y, x]]


class Sems:
    def __init__(self, send, recv):
        self.send, self.recv, self.count = send, recv, 0

    def take(self):
        k = self.count
        self.count += 1
        return self.send.at[k], self.recv.at[k]


def rows_at(start, size):
    return pl.ds(pl.multiple_of(start, TILE), size)


def add_rows(into, one, at, other, other_at, rows):
    step = 32 if rows % 32 == 0 else TILE

    def body(i, carry):
        here = rows_at(at + i * step, step)
        there = rows_at(other_at + i * step, step)
        both = one[here].astype(jnp.float32) + other[there].astype(jnp.float32)
        into[here] = both.astype(into.dtype)
        return carry

    lax.fori_loop(0, rows // step, body, 0)


def sum_item(place, sems, buf, at, rows, order, inbox, used, total, leaving, begun=False):
    z, nz = place.level, place.levels
    above, below = (place.seq + 2, place.batch), (place.seq - 2, place.batch)
    at_end = (z == 0) | (z == nz - 1)
    low, length, held, plan = at, rows, None, []

    def where(condition, act):
        if condition is None:
            act()
        else:
            pl.when(condition)(act)

    def remote(source, into, to):
        return pltpu.make_async_remote_copy(source, into, *sems.take(), device_id=to, device_id_type=MESH_ID)

    def part_of(ref, start, size):
        return ref.at[rows_at(start, size)]

    def chain(up, down, step_up, step_down):
        pl.when(z == 0)(up.start)
        pl.when(z == nz - 1)(down.start)
        yield
        for first, last in hop_groups(nz):
            for hop, copy, step in ((z, up, step_up), (nz - 1 - z, down, step_down)):
                here = (hop >= first) & (hop < last)

                @pl.when(here)
                def _(copy=copy, step=step):
                    copy.wait_recv()
                    step(False)

                @pl.when(here & (hop < nz - 1))
                def _(copy=copy):
                    copy.start()

                @pl.when(here & (hop == nz - 1))
                def _(step=step):
                    step(True)

            if last < nz:
                yield

        def sent():
            pl.when(z < nz - 1)(up.wait_send)
            pl.when(z > 0)(down.wait_send)

        leaving.append(sent)

    for k, axis in enumerate(order):
        last = k == len(order) - 1
        part = length // 2
        if axis == LEVELS:
            ups, downs = low + part, low

            def adder(start, slot, part=part, last=last):
                def step(end):
                    if not last:
                        if not end:
                            add_rows(buf, buf, start, inbox, slot, part)
                    elif end:
                        add_rows(total, buf, start, inbox, slot, part)

                return step

            def adder_last(start, slot, hop, part=part):
                def step(end):
                    if end:
                        add_rows(total, buf, start, inbox, slot, part)
                    else:
                        pl.when(hop < nz - 1)(lambda: add_rows(buf, buf, start, inbox, slot, part))

                return step

            make_up = adder_last(ups, used, z) if last else adder(ups, used)
            make_down = adder_last(downs, used + part, nz - 1 - z) if last else adder(downs, used + part)
            yield from chain(
                remote(part_of(buf, ups, part), part_of(inbox, used, part), above),
                remote(part_of(buf, downs, part), part_of(inbox, used + part, part), below),
                make_up,
                make_down,
            )
            used += 2 * part
            plan.append((axis, low, part, held))
            low = low + jnp.where(z == nz - 1, part, 0)
            held = at_end
        else:
            bit = place.bit(axis)
            keep, give = low + bit * part, low + (1 - bit) * part
            if begun and k == 0:
                plan.append((axis, keep, part, held))
                low, length = keep, part
                continue
            copy = remote(part_of(buf, give, part), part_of(inbox, used, part), place.partner(axis))
            where(held, copy.start)
            yield

            def take(copy=copy, keep=keep, used=used, part=part, last=last):
                copy.wait()
                add_rows(total if last else buf, buf, keep, inbox, used, part)

            where(held, take)
            used += part
            plan.append((axis, keep, part, held))
            low = keep
        length = part
    for axis, low, part, held in reversed(plan):
        if axis == LEVELS:
            ups, downs = part_of(total, low + part, part), part_of(total, low, part)
            nothing = lambda end: None
            yield from chain(remote(downs, downs, above), remote(ups, ups, below), nothing, nothing)
        else:
            here = part_of(total, low, part)
            copy = remote(here, here, place.partner(axis))
            where(held, copy.start)
            yield
            where(held, copy.wait)


def hop_groups(levels):
    groups = min(levels - 1, 3)
    cuts = [1 + (levels - 1) * k // groups for k in range(groups + 1)]
    return list(zip(cuts, cuts[1:]))


def inbox_rows(rows, order, begun):
    used = 0
    for k, axis in enumerate(order):
        rows //= 2
        if begun and k == 0:
            continue
        used += 2 * rows if axis == LEVELS else rows
    return used


def dot(a, b, dims=((1,), (0,))):
    return lax.dot_general(a, b, (dims, ((), ())), preferred_element_type=jnp.float32)


NT = ((1,), (1,))
TN = ((0,), (0,))


def norm_parts(rows):
    center = rows - jnp.mean(rows, axis=-1, keepdims=True)
    spread = jnp.mean(center * center, axis=-1, keepdims=True)
    inverse = lax.rsqrt(spread + norm_eps)
    return center * inverse, inverse


def norm_back(grad, unit, inverse, gain):
    scaled = grad * gain
    along = jnp.mean(scaled * unit, axis=-1, keepdims=True)
    return inverse * (scaled - jnp.mean(scaled, axis=-1, keepdims=True) - unit * along)


def doc_ids(lengths, places):
    found = jnp.zeros(places.shape, jnp.int32)
    end = 0
    for k in range(lengths.shape[1]):
        end += lengths[0, k]
        found += (end <= places).astype(jnp.int32)
    return found


def as_row(ref):
    return ref[...].reshape(1, -1)


def places_down(first, rows):
    return first + lax.broadcasted_iota(jnp.int32, (rows, 1), 0)


def places_along(first, rows):
    return first + lax.broadcasted_iota(jnp.int32, (1, rows), 1)


def mask_of(ends, q_places, k_places):
    allowed = (doc_ids(ends, q_places) == doc_ids(ends, k_places)) & (k_places <= q_places)
    return jnp.where(allowed, 0.0, masked_low)


def first_half():
    return lax.broadcasted_iota(jnp.int32, (1, LANES), 1) < HD


def both_heads(pair):
    left = first_half()
    none = jnp.zeros_like(pair)
    return jnp.concatenate([jnp.where(left, pair, none), jnp.where(left, none, pair)], axis=0)


def own_columns(stacked):
    rows = stacked.shape[0] // 2
    return jnp.where(first_half(), stacked[:rows], stacked[rows:])


def lanes(p):
    return pl.ds(p * LANES, LANES)


def forward_kernel(
    nz, x_ref, e_ref, ends, gain_one1, shift_one1, qkv_bias1, proj_bias1, gain_two1, shift_two1, up_bias1, down_bias1,
    qkv_hbm, proj_hbm, up_hbm, down_hbm,
    layer_out, n1_all, q_out, attn_out, da_out, do_out, n2_out, g_out, du_out, dx_out, stats_out, small_out,
    x_all, qkv_w, proj_w, up_w, down_w, kv, scores, mask, top, total, acc, two_q, res_acc, dh_acc,
    gain_one, shift_one, qkv_bias, proj_bias, gain_two, shift_two, up_bias, down_bias,
    up_send, up_recv, down_send, down_recv, side_send, side_recv, w_sem,
):
    rows, width = x_ref.shape
    pair = 2 * rows
    seq = lax.axis_index("seq")
    batch = lax.axis_index("batch")
    z = seq // 2
    x = seq % 2
    loads = [
        pltpu.make_async_copy(hbm, vmem, w_sem.at[k])
        for k, (hbm, vmem) in enumerate(
            [(qkv_hbm, qkv_w), (proj_hbm, proj_w), (up_hbm, up_w), (down_hbm, down_w)]
        )
    ]
    loads[0].start()
    barrier = pltpu.get_barrier_semaphore()
    has_up = z + 1 < nz
    has_down = z > 0
    above = (seq + 2, batch)
    below = (seq - 2, batch)
    beside = (seq + 1 - 2 * x, batch)

    @pl.when(has_up)
    def _():
        pl.semaphore_signal(barrier, inc=1, device_id=above, device_id_type=MESH_ID)

    @pl.when(has_down)
    def _():
        pl.semaphore_signal(barrier, inc=1, device_id=below, device_id_type=MESH_ID)

    pl.semaphore_signal(barrier, inc=1, device_id=beside, device_id_type=MESH_ID)
    pl.semaphore_wait(barrier, 1 + has_up.astype(jnp.int32) + has_down.astype(jnp.int32))
    for load in loads[1:]:
        load.start()

    half = rows // 2

    def block(level, side, h):
        return x_all.at[rows_at((2 * level + side) * rows + h * half, half)]

    def copies(level, side, to, send_sem, recv_sem, own=False):
        found = []
        for h in range(2):
            source = x_ref.at[h * half : (h + 1) * half] if own else block(level, side, h)
            found.append(
                pltpu.make_async_remote_copy(
                    source, block(level, side, h), send_sem.at[level, h], recv_sem.at[level, h],
                    device_id=to, device_id_type=MESH_ID,
                )
            )
        return found

    def up_copies(level, own=False):
        return copies(level, x, above, up_send, up_recv, own)

    def down_copies(level, own=False):
        return copies(level, x, below, down_send, down_recv, own)

    def side_copies(level, own=False):
        return copies(level, x, beside, side_send, side_recv, own)

    def wait_side(level):
        for copy in copies(level, 1 - x, beside, side_send, side_recv):
            copy.wait_recv()

    own_up, own_side, own_down = up_copies(z, True), side_copies(z, True), down_copies(z, True)
    for h in range(2):

        @pl.when(has_up)
        def _(h=h):
            own_up[h].start()

        own_side[h].start()

        @pl.when(has_down)
        def _(h=h):
            own_down[h].start()

    vectors = [gain_one, shift_one, qkv_bias, proj_bias, gain_two, shift_two, up_bias, down_bias]
    flats = [gain_one1, shift_one1, qkv_bias1, proj_bias1, gain_two1, shift_two1, up_bias1, down_bias1]
    for vector, flat in zip(vectors, flats):
        vector[...] = as_row(flat)
    x_all[rows_at(seq * rows, rows)] = x_ref[...]
    x32 = x_ref[...].astype(jnp.float32)
    unit_one, _ = norm_parts(x32)
    mine = (unit_one * gain_one[...] + shift_one[...]).astype(jnp.bfloat16)
    top[...] = jnp.full(top.shape, masked_low, jnp.float32)
    total[...] = jnp.zeros(total.shape, jnp.float32)
    acc[...] = jnp.zeros(acc.shape, jnp.float32)
    loads[0].wait()
    q = (dot(mine, qkv_w[:, :width]) + qkv_bias[:, :width]).astype(jnp.bfloat16)
    q = q * jnp.asarray(1.0 / math.sqrt(HD), jnp.bfloat16)
    q_out[...] = q
    for p in range(HEADS // 2):
        two_q[p] = both_heads(q[:, p * LANES : (p + 1) * LANES])

    def pass_on(d):
        @pl.when(z >= d)
        def _():
            level = z - d
            ups, sides = up_copies(level), side_copies(level)
            for h in range(2):
                ups[h].wait_recv()

                @pl.when(has_up)
                def _(h=h):
                    ups[h].start()

                sides[h].start()

        @pl.when(z + d < nz)
        def _():
            level = z + d
            downs, sides = down_copies(level), side_copies(level)
            for h in range(2):
                downs[h].wait_recv()

                @pl.when(has_down)
                def _(h=h):
                    downs[h].start()

                sides[h].start()

    def normalize(level):
        here = rows_at(level * pair, pair)
        unit, _ = norm_parts(x_all[here].astype(jnp.float32))
        n1 = (unit * gain_one[...] + shift_one[...]).astype(jnp.bfloat16)
        n1_all[here] = n1
        return n1

    def attend(level):
        wait_side(level)
        n1 = normalize(level)
        kv[...] = (dot(n1, qkv_w[:, width:]) + qkv_bias[:, width:]).astype(jnp.bfloat16)
        one = mask_of(ends, places_down(seq * rows, rows), places_along(level * pair, pair))
        mask[:rows] = one
        mask[rows:] = one
        keeps = []
        for p in range(HEADS // 2):
            s = dot(two_q[p], kv[:, p * LANES : (p + 1) * LANES], NT)
            scores[p] = s
            low = jnp.abs(s) + mask[...]
            before = top[p]
            most = jnp.max(jnp.maximum(low[:, :LANES], low[:, LANES:]), axis=1, keepdims=True)
            newer = jnp.maximum(before, most)
            keeps.append(jnp.exp(before - newer))
            top[p] = newer
        for p in range(HEADS // 2):
            s = scores[p]
            low = mask[...] - jnp.concatenate([top[p], top[p]], axis=1)
            plus = jnp.exp(low + s)
            minus = jnp.exp(low - s)
            both = plus + minus
            total[p] = total[p] * keeps[p] + (both[:, :LANES] + both[:, LANES:])
            v_pair = kv[:, width + p * LANES : width + (p + 1) * LANES]
            out = own_columns(dot((plus - minus).astype(jnp.bfloat16), v_pair))
            here = slice(p * LANES, (p + 1) * LANES)
            acc[:, here] = acc[:, here] * own_columns(keeps[p]) + out

    def level_step(d, carry):
        @pl.when(d + 1 < nz)
        def _():
            pass_on(d + 1)

        @pl.when(z >= d)
        def _():
            attend(z - d)

        @pl.when((d > 0) & (z + d < nz))
        def _():
            wait_side(z + d)
            normalize(z + d)

        return carry

    lax.fori_loop(0, nz, level_step, 0)

    column = lax.broadcasted_iota(jnp.int32, (1, LANES), 1)
    log_total = jnp.zeros((rows, LANES), jnp.float32)
    for p in range(HEADS // 2):
        here = slice(p * LANES, (p + 1) * LANES)
        row_total = jnp.broadcast_to(jnp.sum(total[p], axis=1, keepdims=True), (pair, LANES))
        acc[:, here] = acc[:, here] / own_columns(row_total)
        lse = top[p] + jnp.log(row_total)
        log_total = jnp.where(column == 2 * p, lse[:rows], log_total)
        log_total = jnp.where(column == 2 * p + 1, lse[rows:], log_total)
    attn = acc[...].astype(jnp.bfloat16)
    attn_out[...] = attn
    loads[1].wait()
    resid = x32 + dot(attn, proj_w[...]) + proj_bias[...]
    unit, inverse = norm_parts(resid)
    n2 = (unit * gain_two[...] + shift_two[...]).astype(jnp.bfloat16)
    n2_out[...] = n2
    res_acc[...] = resid + down_bias[...]
    dh_acc[...] = jnp.zeros(dh_acc.shape, jnp.float32)
    loads[2].wait()
    loads[3].wait()
    slope = math.sqrt(2.0 / math.pi)

    def ff_step(t, carry):
        here = pl.ds(pl.multiple_of(t * FF_TILE, FF_TILE), FF_TILE)
        u = dot(n2_out[...], up_w[:, here]) + up_bias[:, here]
        square = u * u
        bend = jnp.tanh(slope * (u + 0.044715 * (square * u)))
        half = 0.5 * (1.0 + bend)
        g = (u * half).astype(jnp.bfloat16)
        slant = half + (0.5 * u) * (1.0 - bend * bend) * (slope * (1.0 + 3.0 * 0.044715 * square))
        g_out[:, here] = g
        res_acc[...] += dot(g, down_w[here])
        du32 = dot(e_ref[...], down_w[here], NT) * slant
        du = du32.astype(jnp.bfloat16)
        du_out[:, here] = du
        small_out[pl.ds(4 + t, 1)] = jnp.sum(du.astype(jnp.float32), axis=0, keepdims=True)
        dh_acc[...] += dot(du, up_w[:, here], NT)
        return carry

    lax.fori_loop(0, up_w.shape[1] // FF_TILE, ff_step, 0)
    layer_out[...] = res_acc[...].astype(jnp.bfloat16)
    dh = dh_acc[...]
    grad_rows = e_ref[...].astype(jnp.float32)
    dx = grad_rows + norm_back(dh, unit, inverse, gain_two[...])
    dx_out[...] = dx
    da = dx.astype(jnp.bfloat16)
    da_out[...] = da
    do = dot(da, proj_w[...], NT).astype(jnp.bfloat16)
    do_out[...] = do
    product = do.astype(jnp.float32) * acc[...]
    delta = jnp.zeros((rows, LANES), jnp.float32)
    left = first_half()
    for p in range(HEADS // 2):
        here = product[:, p * LANES : (p + 1) * LANES]
        one = jnp.sum(jnp.where(left, here, 0.0), axis=1, keepdims=True)
        two = jnp.sum(jnp.where(left, 0.0, here), axis=1, keepdims=True)
        delta = jnp.where(column == 2 * p, one, delta)
        delta = jnp.where(column == 2 * p + 1, two, delta)
    stats_out[0] = log_total
    stats_out[1] = delta
    small_out[0:1] = jnp.sum(dh * unit, axis=0, keepdims=True)
    small_out[1:2] = jnp.sum(dh, axis=0, keepdims=True)
    small_out[2:3] = jnp.sum(grad_rows, axis=0, keepdims=True)
    small_out[3:4] = jnp.sum(da.astype(jnp.float32), axis=0, keepdims=True)

    def left_all(found):
        for copy in found:
            copy.wait_send()

    left_all(side_copies(z, True))

    @pl.when(has_up)
    def _():
        left_all(up_copies(z, True))

    @pl.when(has_down)
    def _():
        left_all(down_copies(z, True))

    def sent(d, carry):
        @pl.when(z >= d)
        def _():
            left_all(side_copies(z - d))

            @pl.when(has_up)
            def _():
                left_all(up_copies(z - d))

        @pl.when(z + d < nz)
        def _():
            left_all(side_copies(z + d))

            @pl.when(has_down)
            def _():
                left_all(down_copies(z + d))

        return carry

    lax.fori_loop(1, nz, sent, 0)


def run_forward(x, e, lengths, gain_one, shift_one, qkv_weight, qkv_bias, proj_weight, proj_bias, gain_two, shift_two, up_weight, up_bias, down_weight, down_bias, peers):
    rows, width = x.shape
    hidden = up_weight.shape[1]
    nz = peers // 2
    bf, f32 = jnp.bfloat16, jnp.float32
    vmem = pl.BlockSpec(memory_space=pltpu.VMEM)
    smem = pl.BlockSpec(memory_space=pltpu.SMEM)
    hbm = pl.BlockSpec(memory_space=pl.ANY)
    dma = pltpu.SemaphoreType.DMA
    outs = [
        ((rows, width), bf), ((peers * rows, width), bf), ((rows, width), bf), ((rows, width), bf), ((rows, width), bf),
        ((rows, width), bf), ((rows, width), bf), ((rows, hidden), bf), ((rows, hidden), bf), ((rows, width), f32),
        ((2, rows, LANES), f32), ((4 + hidden // width, width), f32),
    ]
    vectors = [gain_one, shift_one, qkv_bias, proj_bias, gain_two, shift_two, up_bias, down_bias]
    return pl.pallas_call(
        functools.partial(forward_kernel, nz),
        out_shape=[(pltpu.VMEM if fits(peers, rows) and k in KEPT else jax.ShapeDtypeStruct)(*o) for k, o in enumerate(outs)],
        in_specs=[vmem, vmem, smem] + [vmem] * 8 + [hbm] * 4,
        out_specs=[vmem] * len(outs),
        scratch_shapes=[
            pltpu.VMEM((peers * rows, width), bf),
            pltpu.VMEM(qkv_weight.shape, bf),
            pltpu.VMEM(proj_weight.shape, bf),
            pltpu.VMEM(up_weight.shape, bf),
            pltpu.VMEM(down_weight.shape, bf),
            pltpu.VMEM((2 * rows, 2 * width), bf),
            pltpu.VMEM((HEADS // 2, 2 * rows, 2 * rows), f32),
            pltpu.VMEM((2 * rows, 2 * rows), f32),
            pltpu.VMEM((HEADS // 2, 2 * rows, LANES), f32),
            pltpu.VMEM((HEADS // 2, 2 * rows, LANES), f32),
            pltpu.VMEM((rows, width), f32),
            pltpu.VMEM((HEADS // 2, 2 * rows, LANES), bf),
            pltpu.VMEM((rows, width), f32),
            pltpu.VMEM((rows, width), f32),
            *[pltpu.VMEM((1, v.shape[0]), f32) for v in vectors],
            *[dma((nz, 2))] * 6, dma((4,)),
        ],
        compiler_params=pltpu.CompilerParams(collective_id=0, has_side_effects=True, vmem_limit_bytes=60 * 2**20),
        cost_estimate=pl.CostEstimate(flops=10**9, bytes_accessed=2 * 10**7, transcendentals=10**6),
    )(x, e, lengths, *vectors, qkv_weight, proj_weight, up_weight, down_weight)


def backward_kernel(
    nz, items, orders, schedule,
    x_ref, e_ref, ends, gain_flat, bias_flat, n1_all, q_ref, attn_ref, da_ref, do_ref, n2_ref, g_ref, du_ref, dx_ref,
    stats_ref, first_small, qkv_hbm,
    input_grad, qkv_out, proj_out, up_out, down_out, small_out,
    qkv_w, buf, inbox, total, do_all, rows_all, g_cat, e_cat, n2_cat, du_cat, attn_cat, da_cat, n1_cat, dqkv_cat,
    two_q, two_do, two_k, two_v, lse_cols, delta_cols, kv, n1_held, mask, dq, dk, dv, small_in, gain_one, qkv_bias,
    e_far, g_far, n2_far, du_far,
    down_send, down_recv, side_send, side_recv, ssem, rsem, lsem,
):
    rows, width = x_ref.shape
    pair = 2 * rows
    place = Place()
    seq, batch = place.seq, place.batch
    z = seq // 2
    x = seq % 2
    core = place.bit(CORE)
    sems = Sems(ssem, rsem)
    local = Sems(lsem, lsem)
    load = pltpu.make_async_copy(qkv_hbm, qkv_w, local.take()[0])
    load.start()
    small_axes = [CORE, ACROSS] + seq_axes(2 * nz)
    has_up = z + 1 < nz
    has_down = z > 0
    above = (seq + 2, batch)
    below = (seq - 2, batch)
    beside = (seq + 1 - 2 * x, batch)
    barrier = pltpu.get_barrier_semaphore()
    for axis in small_axes:
        pl.semaphore_signal(barrier, inc=1, device_id=place.partner(axis), device_id_type=MESH_ID)

    @pl.when(has_up)
    def _():
        pl.semaphore_signal(barrier, inc=1, device_id=above, device_id_type=MESH_ID)

    @pl.when(has_down)
    def _():
        pl.semaphore_signal(barrier, inc=1, device_id=below, device_id_type=MESH_ID)

    gain_one[...] = as_row(gain_flat)
    qkv_bias[...] = as_row(bias_flat)
    for k in range(2):
        rows_all[seq, k * TILE : (k + 1) * TILE] = stats_ref[k].T[:TILE]
    pl.semaphore_wait(barrier, len(small_axes) + has_up.astype(jnp.int32) + has_down.astype(jnp.int32))

    def cols(half, size):
        return pl.ds(pl.multiple_of(half * size, LANES), size)

    def to_core(source, into):
        return pltpu.make_async_remote_copy(
            source, into.at[rows:], *sems.take(), device_id=place.partner(CORE), device_id_type=MESH_ID
        )

    def keep_own(source, into):
        return pltpu.make_async_copy(source, into.at[:rows], local.take()[0])

    def exchange(ref, into, halved):
        size = into.shape[1]
        give = ref.at[:, cols(1 - core, size)] if halved else ref
        keep = ref.at[:, cols(core, size)] if halved else ref
        copies = [to_core(give, into), keep_own(keep, into)]
        for copy in copies:
            copy.start()
        return copies

    def done(copies):
        for copy in copies:
            copy.wait()

    down_parts = exchange(g_ref, g_cat, True) + exchange(e_ref, e_cat, False)
    up_parts = exchange(n2_ref, n2_cat, False) + exchange(du_ref, du_cat, True)

    def do_block(level, side):
        return do_all.at[rows_at((2 * level + side) * rows, rows)]

    def do_copies(level, side, to, send_sem, recv_sem, own=False):
        source = do_ref if own else do_block(level, side)
        stat = rows_all.at[2 * level + side]
        return [
            pltpu.make_async_remote_copy(
                source, do_block(level, side), send_sem.at[level, 0], recv_sem.at[level, 0], device_id=to, device_id_type=MESH_ID
            ),
            pltpu.make_async_remote_copy(
                stat, stat, send_sem.at[level, 1], recv_sem.at[level, 1], device_id=to, device_id_type=MESH_ID
            ),
        ]

    def down_copies(level, own=False):
        return do_copies(level, x, below, down_send, down_recv, own)

    def side_copies(level, own=False):
        return do_copies(level, x, beside, side_send, side_recv, own)

    def begin(copies):
        for copy in copies:
            copy.start()

    @pl.when(has_down)
    def _():
        begin(down_copies(z, True))

    begin(side_copies(z, True))
    do_all[rows_at(seq * rows, rows)] = do_ref[...]

    spread = [1]

    def spread_until(last):
        while spread[0] <= min(last, nz - 1):
            d = spread[0]
            spread[0] += 1

            @pl.when(z + d < nz)
            def _():
                level = z + d
                for copy in down_copies(level):
                    copy.wait_recv()

                @pl.when(has_down)
                def _():
                    begin(down_copies(level))

                begin(side_copies(level))

    def spread_end():
        def sent(copies):
            for copy in copies:
                copy.wait_send()

        sent(side_copies(z, True))

        @pl.when(has_down)
        def _():
            sent(down_copies(z, True))

        def each(level, carry):
            sent(side_copies(level))

            @pl.when(has_down)
            def _():
                sent(down_copies(level))

            return carry

        lax.fori_loop(z + 1, nz, each, 0)

    slots = []
    at = used = 0
    for size, kind, (name, _) in items:
        slots.append((at, size, orders[kind], used))
        at += size
        used += inbox_rows(size, orders[kind], name in FAR)
    places = [(name, r) for _, _, (name, r) in items]

    def destination(name, r, size):
        half = width // 2
        if name == "down":
            return down_out.at[rows_at(core * down_out.shape[0] // 2 + r, size)]
        if name == "up":
            return up_out.at[rows_at(core * up_out.shape[0] // 2 + r, size)]
        if name == "proj":
            return proj_out.at[rows_at(core * half + r, size)]
        return qkv_out.at[rows_at(core * half + r, size), int(name[3:]) * width : (int(name[3:]) + 1) * width]

    ready = set()

    def item_task(k):
        at, size, order, used = slots[k]
        name, r = places[k]
        begun = name[:2] in far
        if begun:
            axis, left, right, left_far, right_far, copy, columns = far[name[:2]]
            if name[:2] not in ready:
                ready.add(name[:2])
                share(copy, right_far)
            part = size // 2
            n = r // size
            columns[n].wait()
            mine = left[:, pl.ds(pl.multiple_of(r + place.bit(axis) * part, LANES), part)]
            both = dot(mine, right[...], TN) + dot(left_far[:, n * part : (n + 1) * part], right_far[...], TN)
            buf[rows_at(at + place.bit(axis) * part, part)] = both.astype(jnp.bfloat16)
        else:
            if name[:2] not in ready:
                ready.add(name[:2])
                done(parts[name[:2]])
            left, right = operands(name)
            buf[at : at + size] = dot(left[:, r : r + size], right, TN).astype(jnp.bfloat16)
        yield from sum_item(place, sems, buf, at, size, order, inbox, used, total, ending, begun)
        there = destination(name, r, size)
        here = total.at[rows_at(at, size)]
        keep = pltpu.make_async_copy(here, there, local.take()[0])
        give = pltpu.make_async_remote_copy(here, there, *sems.take(), device_id=place.partner(CORE), device_id_type=MESH_ID)
        keep.start()
        give.start()
        leaving.extend([keep, give])

    def small_task():
        for k, axis in enumerate(small_axes):
            copy = pltpu.make_async_remote_copy(
                small_out, small_in.at[k], *sems.take(), device_id=place.partner(axis), device_id_type=MESH_ID
            )
            copy.start()
            yield
            copy.wait()
            small_out[...] += small_in[k]

    leaving, ending = [], []

    def operands(name):
        if name == "proj":
            return attn_cat, da_cat[...]
        j = int(name[-1])
        block = slice(j * width, (j + 1) * width)
        return n1_cat, dqkv_cat[:, block]

    x_axis = ("seq", 0)

    def far_start(ref, into, axis):
        copy = pltpu.make_async_remote_copy(
            ref, into.at[:rows], *sems.take(), device_id=place.partner(axis), device_id_type=MESH_ID
        )
        copy.start()
        return copy

    def far_columns(cat, into, axis):
        copies = []
        for n in range(into.shape[1] // LANES):
            columns = pl.ds(pl.multiple_of((2 * n + 1 - place.bit(axis)) * LANES, LANES), LANES)
            copy = pltpu.make_async_remote_copy(
                cat.at[:, columns], into.at[:, n * LANES : (n + 1) * LANES], *sems.take(),
                device_id=place.partner(axis), device_id_type=MESH_ID,
            )
            copy.start()
            copies.append(copy)
        return copies

    def share(copy, into):
        copy.wait()
        other = pltpu.make_async_remote_copy(
            into.at[:rows], into.at[rows:], *sems.take(), device_id=place.partner(CORE), device_id_type=MESH_ID
        )
        other.start()
        other.wait()

    e_copy = far_start(e_ref, e_far, ACROSS)
    n2_copy = far_start(n2_ref, n2_far, x_axis)
    done(down_parts)
    done(up_parts)
    far = {
        "do": (ACROSS, g_cat, e_cat, g_far, e_far, e_copy, far_columns(g_cat, g_far, ACROSS)),
        "up": (x_axis, du_cat, n2_cat, du_far, n2_far, n2_copy, far_columns(du_cat, du_far, x_axis)),
    }
    small_out[:8] = first_small[...]
    own_n1 = rows_at(seq * rows, rows)
    parts = {
        "pr": exchange(attn_ref, attn_cat, True) + exchange(da_ref, da_cat, False),
        "qk": exchange(n1_all.at[own_n1], n1_cat, True),
    }

    load.wait()
    scale = jnp.asarray(1.0 / math.sqrt(HD), jnp.bfloat16)

    chunk_sem = local.take()[0]

    def n1_chunk(level):
        copy = pltpu.make_async_copy(n1_all.at[rows_at(level * pair, pair)], n1_held, chunk_sem)
        copy.start()
        copy.wait()
        return n1_held[...]

    def prepare():
        n1_chunk(z)
        mine = n1_held[rows_at(x * rows, rows)]
        own_kv = (dot(mine, qkv_w[:, width:]) + qkv_bias[:, width:]).astype(jnp.bfloat16)
        for p in range(HEADS // 2):
            here = slice(p * LANES, (p + 1) * LANES)
            two_q[p] = both_heads(q_ref[:, here])
            two_do[p] = both_heads(do_ref[:, here])
            two_k[p] = both_heads(own_kv[:, here])
            two_v[p] = both_heads(own_kv[:, width + p * LANES : width + (p + 1) * LANES])
            for k, into in enumerate((lse_cols, delta_cols)):
                for h in range(2):
                    column = stats_ref[k, :, 2 * p + h : 2 * p + h + 1]
                    into[p, h * rows : (h + 1) * rows] = jnp.broadcast_to(column, (rows, LANES))
        dq[...] = jnp.zeros(dq.shape, jnp.float32)
        dk[...] = jnp.zeros(dk.shape, jnp.float32)
        dv[...] = jnp.zeros(dv.shape, jnp.float32)

    def columns_of(p):
        return pl.ds(pl.multiple_of(p * LANES, LANES), LANES)

    def query_step(level):
        n1 = n1_chunk(level)
        kv[...] = (dot(n1, qkv_w[:, width:]) + qkv_bias[:, width:]).astype(jnp.bfloat16)
        one = mask_of(ends, places_down(seq * rows, rows), places_along(level * pair, pair))
        mask[:rows] = one
        mask[rows:] = one

        def each(p, carry):
            k_pair = kv[:, columns_of(p)]
            v_pair = kv[:, columns_of(p + HEADS // 2)]
            s = dot(two_q[p], k_pair, NT)
            along = dot(two_do[p], v_pair, NT)
            low = mask[...] - lse_cols[p][:, :1]
            plus = jnp.exp(low + s)
            minus = jnp.exp(low - s)
            ds = ((plus + minus) * along - (plus - minus) * delta_cols[p][:, :1]).astype(jnp.bfloat16)
            dq[:, columns_of(p)] += own_columns(dot(ds, k_pair))
            return carry

        lax.fori_loop(0, HEADS // 2, each, 0, unroll=UNROLL)

    def key_step(level):
        side = 1 - x
        for copy in do_copies(level, side, beside, side_send, side_recv):
            copy.wait_recv()
        here = rows_at(level * pair, pair)
        n1 = n1_chunk(level)
        kv[:, :width] = (dot(n1, qkv_w[:, :width]) + qkv_bias[:, :width]).astype(jnp.bfloat16) * scale
        one = mask_of(ends, places_along(level * pair, pair), places_down(seq * rows, rows))
        mask[:rows] = one
        mask[rows:] = one

        def stat(row):
            both = [rows_all[2 * level + k, pl.ds(row, 1)] for k in range(2)]
            return jnp.concatenate(both, axis=1)

        def stat_rows(k, p):
            both = [jnp.broadcast_to(stat(k * TILE + 2 * p + h), (rows, pair)) for h in range(2)]
            return jnp.concatenate(both, axis=0)

        def each(p, carry):
            q_pair = kv[:, columns_of(p)]
            do_pair = do_all[here, columns_of(p)]
            s = dot(two_k[p], q_pair, NT)
            along = dot(two_v[p], do_pair, NT)
            low = mask[...] - stat_rows(0, p)
            plus = jnp.exp(low + s)
            minus = jnp.exp(low - s)
            signed = plus - minus
            ds = ((plus + minus) * along - signed * stat_rows(1, p)).astype(jnp.bfloat16)
            dk[:, columns_of(p)] += own_columns(dot(ds, q_pair))
            dv[:, columns_of(p)] += own_columns(dot(signed.astype(jnp.bfloat16), do_pair))
            return carry

        lax.fori_loop(0, HEADS // 2, each, 0, unroll=UNROLL)

    def one_step(t):
        @pl.when(t <= z)
        def _():
            query_step(z - t)

        @pl.when(t > z)
        def _():
            key_step(t - 1)

    def steps_piece(first, last):
        def piece():
            spread_until(last)
            if last - first == 1:
                one_step(first)
            else:

                def body(t, carry):
                    one_step(t)
                    return carry

                lax.fori_loop(first, last, body, 0)

        return piece

    def finish():
        dqkv = jnp.concatenate(
            [
                (dq[...] * (1.0 / math.sqrt(HD))).astype(jnp.bfloat16),
                dk[...].astype(jnp.bfloat16),
                dv[...].astype(jnp.bfloat16),
            ],
            axis=1,
        )
        dqkv_cat[:rows] = dqkv
        send = to_core(dqkv_cat.at[:rows], dqkv_cat)
        send.start()
        dh = dot(dqkv, qkv_w[...], NT)
        unit, inverse = norm_parts(x_ref[...].astype(jnp.float32))
        input_grad[...] = (dx_ref[...] + norm_back(dh, unit, inverse, gain_one[...])).astype(jnp.bfloat16)
        sums = jnp.sum(dqkv.astype(jnp.float32), axis=0, keepdims=True)
        for k in range(3):
            small_out[8 + k : 9 + k] = sums[:, k * width : (k + 1) * width]
        small_out[11:12] = jnp.sum(dh * unit, axis=0, keepdims=True)
        small_out[12:13] = jnp.sum(dh, axis=0, keepdims=True)
        small_out[13:16] = jnp.zeros((3, width), jnp.float32)
        parts["qk"].append(send)

    groups = min(nz + 1, GROUPS)
    cuts = [(nz + 1) * k // groups for k in range(groups + 1)]
    pieces = [prepare] + [steps_piece(a, b) for a, b in zip(cuts, cuts[1:])] + [finish]
    tasks = [item_task(k) for k in range(len(items))] + [small_task()]
    for token in schedule:
        if token < 0:
            pieces[-1 - token]()
        else:
            next(tasks[token], None)
    for copy in leaving:
        copy.wait()
    for sent in ending:
        sent()
    spread_end()


def in_turns(items, counts, n_pieces):
    early = [k for k, (_, _, (name, _)) in enumerate(items) if name[:3] != "qkv"]
    late = [k for k in range(len(counts)) if k not in early]
    tokens, piece = [], 0
    for waiting in (early, late):
        live = []
        while live or waiting:
            live, waiting = live + waiting[:3], waiting[3:]
            for k in live:
                tokens.append(k)
                if len(tokens) % PACE == 0 and piece < n_pieces:
                    piece += 1
                    tokens.append(-piece)
            live = [k for k in live if tokens.count(k) < counts[k]]
        while piece < n_pieces:
            piece += 1
            tokens.append(-piece)
    return tokens


def fits(peers, rows):
    return peers * rows <= 2048


def plan_items(width, hidden):
    half = width // 2

    def cut(name, size):
        return [(min(ITEM, size - r), (name, r)) for r in range(0, size, ITEM)]

    found = cut("down", hidden // 2)
    found += cut("up", hidden // 2)
    found += cut("proj", half)
    for j in range(3):
        found += cut(f"qkv{j}", half)
    return [(size, int(KINDS[k % len(KINDS)]), where) for k, (size, where) in enumerate(found)]


def run_backward(x, e, lengths, gain_one, qkv_weight, qkv_bias, kept, peers):
    n1_all, q, attn, da, do, n2, g, du, dx, stats, small = kept
    rows, width = x.shape
    hidden = g.shape[1]
    nz = peers // 2
    bf, f32 = jnp.bfloat16, jnp.float32
    orders = axis_orders()
    stages = 2 + len(seq_axes(peers))
    items = plan_items(width, hidden)
    used = sum(inbox_rows(size, orders[kind], name in FAR) for size, kind, (name, _) in items)
    height = sum(size for size, _, _ in items)
    turns = [1 + 2 * (2 + len(hop_groups(nz))) - (name in FAR) for _, _, (name, _) in items] + [1 + stages]
    n_pieces = 2 + min(nz + 1, GROUPS)
    schedule = SCHEDULE
    if sorted(schedule) != sorted([k for k, n in enumerate(turns) for _ in range(n)] + [-1 - k for k in range(n_pieces)]):
        schedule = in_turns(items, turns, n_pieces)
    copies = 9 * len(items) + stages + 8 + 4 + hidden // LANES // 2
    vmem = pl.BlockSpec(memory_space=pltpu.VMEM)
    smem = pl.BlockSpec(memory_space=pltpu.SMEM)
    hbm = pl.BlockSpec(memory_space=pl.ANY)
    dma = pltpu.SemaphoreType.DMA
    out = jax.ShapeDtypeStruct
    small_mesh = fits(peers, rows)
    grad = pltpu.VMEM if small_mesh else out
    stack = (HEADS // 2, 2 * rows, LANES)
    return pl.pallas_call(
        functools.partial(backward_kernel, nz, items, orders, schedule),
        out_shape=[
            grad((rows, width), bf), grad((width, 3 * width), bf), grad((width, width), bf), grad((hidden, width), bf),
            grad((hidden, width), bf), out((16, width), f32),
        ],
        in_specs=[vmem, hbm, smem, vmem, vmem]
        + [vmem if k in (2, 5, 9, 10, 11) or (small_mesh and k in KEPT) else hbm for k in range(1, 12)]
        + [hbm],
        out_specs=[vmem] + [vmem if small_mesh else hbm] * 4 + [vmem],
        scratch_shapes=[
            pltpu.VMEM(qkv_weight.shape, bf),
            pltpu.VMEM((height, width), bf),
            pltpu.VMEM((used, width), bf),
            pltpu.VMEM((height, width), bf),
            pltpu.VMEM((peers * rows, width), bf),
            pltpu.VMEM((peers, 2 * TILE, LANES), f32),
            pltpu.VMEM((2 * rows, hidden // 2), bf),
            pltpu.VMEM((2 * rows, width), bf),
            pltpu.VMEM((2 * rows, width), bf),
            pltpu.VMEM((2 * rows, hidden // 2), bf),
            pltpu.VMEM((2 * rows, width // 2), bf),
            pltpu.VMEM((2 * rows, width), bf),
            pltpu.VMEM((2 * rows, width // 2), bf),
            pltpu.VMEM((2 * rows, 3 * width), bf),
            pltpu.VMEM(stack, bf), pltpu.VMEM(stack, bf), pltpu.VMEM(stack, bf), pltpu.VMEM(stack, bf),
            pltpu.VMEM(stack, f32), pltpu.VMEM(stack, f32),
            pltpu.VMEM((2 * rows, 2 * width), bf),
            pltpu.VMEM((2 * rows, width), bf),
            pltpu.VMEM((2 * rows, 2 * rows), f32),
            pltpu.VMEM((rows, width), f32), pltpu.VMEM((rows, width), f32), pltpu.VMEM((rows, width), f32),
            pltpu.VMEM((stages, 16, width), f32),
            pltpu.VMEM((1, width), f32), pltpu.VMEM((1, 3 * width), f32),
            pltpu.VMEM((2 * rows, width), bf), pltpu.VMEM((2 * rows, hidden // 4), bf),
            pltpu.VMEM((2 * rows, width), bf), pltpu.VMEM((2 * rows, hidden // 4), bf),
            dma((nz, 2)), dma((nz, 2)), dma((nz, 2)), dma((nz, 2)),
            dma((copies,)), dma((copies,)), dma((len(items) + 10,)),
        ],
        compiler_params=pltpu.CompilerParams(collective_id=1, has_side_effects=True, vmem_limit_bytes=(K2_LIMIT if small_mesh else 62) * 2**20),
    )(x, e, lengths, gain_one, qkv_bias, n1_all, q, attn, da, do, n2, g, du, dx, stats, small, qkv_weight)


def widen_kernel(grads, small, passed, outs, rests, passed_outs, slots, sems, pass_sems):
    moved = [pltpu.make_async_copy(a, b, pass_sems.at[k]) for k, (a, b) in enumerate(zip(passed, passed_outs))]
    for copy in moved:
        copy.start()
    for k, (grad, out) in enumerate(zip(grads, outs)):
        slot = slots[k]
        turned = k == TURNED
        rows = slot.shape[2] if turned else slot.shape[1]
        flying = []
        for n in range(grad.shape[0] // rows):
            at = n % slot.shape[0]
            if len(flying) >= slot.shape[0]:
                flying[n - slot.shape[0]].wait()

            def body(i, carry, n=n, at=at, grad=grad, slot=slot, rows=rows):
                here = pl.ds(pl.multiple_of(i * TILE, TILE), TILE)
                there = pl.ds(pl.multiple_of(n * rows + i * TILE, TILE), TILE)
                slot[at, here] = grad[there].astype(jnp.float32)
                return carry

            def turn(i, carry, n=n, at=at, grad=grad, slot=slot, rows=rows):
                here = pl.ds(pl.multiple_of(i * LANES, LANES), LANES)
                there = pl.ds(pl.multiple_of(n * rows + i * LANES, LANES), LANES)
                for c in range(0, grad.shape[1], LANES):
                    slot[at, c : c + LANES, here] = grad[there, c : c + LANES].astype(jnp.float32).T
                return carry

            if turned:
                lax.fori_loop(0, rows // LANES, turn, 0)
            else:
                lax.fori_loop(0, rows // TILE, body, 0)
            into = out.at[:, n * rows : (n + 1) * rows] if turned else out.at[n * rows : (n + 1) * rows]
            copy = pltpu.make_async_copy(slot.at[at], into, sems.at[k, n % slot.shape[0]])
            copy.start()
            flying.append(copy)
        moved += flying[-slot.shape[0] :]
    for (first, count), rest in zip(SMALL_ROWS, rests):
        for k in range(count):
            rest[k * small.shape[1] : (k + 1) * small.shape[1]] = small[first + k : first + k + 1].reshape(small.shape[1])
    for copy in moved:
        copy.wait()


def widen(grads, small, passed):
    width = small.shape[1]
    depth = 3
    sizes = [(g.shape, max(TILE, WIDEN // g.shape[1] // TILE * TILE)) for g in grads]
    vmem = pl.BlockSpec(memory_space=pltpu.VMEM)
    hbm = pl.BlockSpec(memory_space=pl.ANY)
    n = len(grads)
    m = len(SMALL_ROWS)
    q = len(passed)

    def kernel(*refs):
        found = []
        for count in (n, 1, q, n, m, q, n):
            found.append(refs[:count])
            refs = refs[count:]
        found[1] = found[1][0]
        widen_kernel(*found, *refs)

    return pl.pallas_call(
        kernel,
        out_shape=[jax.ShapeDtypeStruct(g.shape[::-1] if k == TURNED else g.shape, jnp.float32) for k, g in enumerate(grads)]
        + [jax.ShapeDtypeStruct((count * width,), jnp.float32) for _, count in SMALL_ROWS]
        + [jax.ShapeDtypeStruct(p.shape, p.dtype) for p in passed],
        in_specs=[vmem] * (n + 1) + [vmem] * q,
        out_specs=[hbm] * n + [vmem] * m + [hbm] * q,
        scratch_shapes=[
            pltpu.VMEM((depth, shape[1], rows) if k == TURNED else (depth, rows, shape[1]), jnp.float32)
            for k, (shape, rows) in enumerate(sizes)
        ]
        + [pltpu.SemaphoreType.DMA((n, depth)), pltpu.SemaphoreType.DMA((q,))],
        compiler_params=pltpu.CompilerParams(vmem_limit_bytes=34 * 2**20),
    )(*grads, small, *passed)


def per_device(
    inputs,
    cotangent,
    doc_lengths,
    gain_one,
    shift_one,
    qkv_weight,
    qkv_bias,
    proj_weight,
    proj_bias,
    gain_two,
    shift_two,
    up_weight,
    up_bias,
    down_weight,
    down_bias,
):
    peers = lax.axis_size("seq")
    width = inputs.shape[2]
    layer_out, *kept = run_forward(
        inputs[0], cotangent[0], doc_lengths, gain_one, shift_one, qkv_weight, qkv_bias, proj_weight, proj_bias, gain_two, shift_two,
        up_weight, up_bias, down_weight, down_bias, peers,
    )
    input_grad, qkv, proj, up, down, small = run_backward(
        inputs[0], cotangent[0], doc_lengths, gain_one, qkv_weight, qkv_bias, kept, peers
    )
    large = (qkv, proj, up, down)
    if fits(peers, inputs.shape[1]):
        qkv, proj, up, down, *rest, layer_out, input_grad = widen(large, small, (layer_out, input_grad))
    else:
        qkv, proj, up, down = (g.astype(jnp.float32) for g in (qkv, proj, up.T, down))
        rest = [small[first : first + count].reshape(-1) for first, count in SMALL_ROWS]
    gain_1, shift_1, qkv_b, proj_b, gain_2, shift_2, up_b, down_b = rest
    return (
        layer_out[None], input_grad[None], gain_1, shift_1, qkv, qkv_b, proj, proj_b, gain_2, shift_2, up, up_b, down, down_b,
    )


def solution(mesh):
    in_specs = (
        P("batch", "seq", None),
        P("batch", "seq", None),
        P("batch", None),
        P(),
        P(),
        P(),
        P(),
        P(),
        P(),
        P(),
        P(),
        P(),
        P(),
        P(),
        P(),
    )
    out_specs = (
        P("batch", "seq", None),
        P("batch", "seq", None),
        P(),
        P(),
        P(),
        P(),
        P(),
        P(),
        P(),
        P(),
        P(),
        P(),
        P(),
        P(),
    )
    return jax.shard_map(
        per_device, mesh=mesh, in_specs=in_specs, out_specs=out_specs, check_vma=False
    )
```

profile of v0, /device:TPU:0, one launch (start us, length us, event | category | flops | bytes accessed | tf_op | source)
XLA Modules:
  0.0 169.5 jit_solution(5192210213459447570)
XLA Ops:
  0.6 33.7 %shard_map.254 = (bf16[128,768]{1,0:T(8,128)(2,1)S(1)}, bf16[1024,768]{1,0:T(8,128)(2,1)}, bf16[128,768]{1,0:T(8,128)(2,1)}, bf16[128,768]{1,0:T(8,128)(2,1)}, b...) custom-call(bf16[128,768]{1,0:T(8,128)(2,1)} %bitcast.4, ...), custom_call_target="tpu_custom_call" | custom-call | flops 1000000000 | bytes 20000000 | tf_op jit(solution)/shard_map/pallas_call | solution.py:604
  34.4 122.8 %shard_map.255 = (bf16[128,768]{1,0:T(8,128)(2,1)S(1)}, bf16[768,2304]{1,0:T(8,128)(2,1)S(1)}, bf16[768,768]{1,0:T(8,128)(2,1)S(1)}, bf16[3072,768]{1,0:T(8,128)...) custom-call(bf16[128,768]{1,0:T(8,128)(2,1)} %bitcast.5, bf16[128,768]{1,0:T(8,128)(2,1)} %bitcast.7, ...), custom_call_target="tpu_custom_call" | custom-call | tf_op jit(solution)/shard_map/pallas_call | solution.py:1104
  157.2 0.0 copy-start
  157.2 0.8 copy-done
  158.0 11.3 %shard_map.256 = (f32[768,2304]{1,0:T(8,128)}, f32[768,768]{1,0:T(8,128)}, f32[768,3072]{1,0:T(8,128)}, f32[3072,768]{1,0:T(8,128)}, f32[768]{0:T(1024)}, /*inde...) custom-call(bf16[768,2304]{1,0:T(8,128)(2,1)S(1)} %get-tuple-element, ...), custom_call_target="tpu_custom_call" | custom-call | tf_op jit(solution)/shard_map/pallas_call | solution.py:1207
Async XLA Ops:
  157.2 0.8 copy-start
where the time goes:
time: 170 us; the launch traced here: 169 us
  Pallas kernels  168 us (99%)
    pallas_call x1, Pallas kernels, run_backward(): pl.pallas_call(functools.partial(backward_kernel, nz, items, orders, sche...  123 us
    pallas_call x1, Pallas kernels, run_forward(): pl.pallas_call(functools.partial(forward_kernel, nz), out_shape=[(pltpu.V...  33.7 us
    pallas_call x1, Pallas kernels, widen(): pl.pallas_call(kernel, out_shape=[jax.ShapeDtypeStruct(g.shape[::-1] if k...  11.3 us

commit v1 on v0

--- a/solution.py
+++ b/solution.py
@@ -21,7 +21,7 @@
 LANES = 128
 FF_TILE = 768
 ITEM = 256
-KINDS = "11133300404055354145"
+KINDS = "13111140004435354202"
 GROUPS = 5
 PACE = 8
 UNROLL = 2
@@ -32,13 +32,13 @@
 WIDEN = 128 * 2304
 SMALL_ROWS = ((11, 1), (12, 1), (8, 3), (3, 1), (0, 1), (1, 1), (4, 4), (2, 1))
 SCHEDULE = (
-    -1, 12, -2, 13, 12, 0, 6, 13, -3, 12, 6, 0, 1, 2, 9, 10, 11, 13, 6, 8, 7, -4, 6, 11, 10, 4, 12, 0, 3, 2, 5, 6, 7,
-    -5, 2, 9, 1, 13, 12, 11, -6, 9, 2, 1, 4, 6, 8, 3, 10, -7, 18, 4, 19, 6, 14, 5, 3, 8, 16, 1, 7, 10, 9, 6, 19, 7, 4,
-    15, 18, 12, 17, 5, 3, 20, 15, 11, 0, 7, 9, 20, 14, 5, 18, 3, 2, 16, 7, 15, 4, 9, 13, 3, 19, 16, 10, 7, 5, 18, 5,
-    6, 17, 8, 17, 12, 14, 15, 2, 1, 19, 7, 16, 13, 10, 15, 14, 20, 18, 3, 8, 14, 16, 0, 18, 17, 2, 7, 10, 1, 15, 11,
-    9, 2, 14, 13, 16, 19, 17, 5, 9, 18, 1, 3, 0, 2, 4, 19, 8, 17, 7, 14, 18, 11, 15, 10, 20, 5, 0, 14, 19, 9, 4, 3,
-    18, 16, 15, 14, 19, 13, 16, 5, 4, 1, 10, 1, 8, 11, 3, 16, 15, 11, 8, 12, 0, 5, 17, 18, 15, 8, 9, 19, 10, 12, 14,
-    20, 17, 11, 4, 12, 13, 16, 0, 14, 17, 20, 15, 8, 13, 19, 12, 6, 4, 17, 16, 0, 17, 18, 11, 19, 13, 1, 2,
+    -1, 13, -2, 2, 0, 7, 13, 2, 12, 5, 3, -3, 7, 0, 10, 9, 6, 8, 0, 3, 4, 10, -4, 8, 5, 7, 6, 11, 2, 0, 3, 4, 9, 1,
+    13, -5, 7, 12, 11, 10, 2, -6, 6, 0, 1, 1, 8, 11, -7, 5, 16, 9, 12, 13, 8, 3, 15, 10, 2, 14, 1, 6, 15, 9, 17, 10,
+    20, 17, 13, 18, 19, 7, 15, 11, 19, 1, 13, 12, 4, 16, 20, 14, 9, 7, 1, 11, 15, 8, 19, 5, 7, 10, 9, 20, 1, 8, 0, 18,
+    14, 15, 16, 9, 13, 17, 4, 10, 19, 6, 11, 7, 1, 16, 14, 5, 9, 2, 8, 19, 11, 18, 10, 15, 17, 3, 12, 1, 14, 5, 16, 4,
+    19, 7, 3, 15, 6, 20, 2, 10, 18, 14, 2, 17, 18, 8, 11, 16, 12, 3, 4, 6, 2, 5, 19, 14, 8, 15, 16, 3, 7, 1, 13, 18,
+    0, 19, 11, 17, 4, 3, 5, 5, 9, 20, 0, 12, 14, 13, 4, 17, 10, 12, 6, 8, 14, 0, 9, 18, 16, 13, 15, 17, 12, 4, 18, 6,
+    16, 3, 18, 17, 12, 15, 16, 2, 15, 6, 0, 20, 17, 5, 19, 14, 13, 19, 18, 16, 17, 12, 4, 14, 18, 11, 19,
 )
 
 
@@ -1188,7 +1188,7 @@
 
 def widen(grads, small, passed):
     width = small.shape[1]
-    depth = 3
+    depth = 4
     sizes = [(g.shape, max(TILE, WIDEN // g.shape[1] // TILE * TILE)) for g in grads]
     vmem = pl.BlockSpec(memory_space=pltpu.VMEM)
     hbm = pl.BlockSpec(memory_space=pl.ANY)

time: 170 us -> 167 us (0.982)
  Pallas kernels: 168 us -> 165 us
    pallas_call x1, Pallas kernels: 123 us -> 121 us  [run_backward(): pl.pallas_call(functools.partial(backward_kernel, nz, items, orders, sche...]
where the time goes in v1:
time: 167 us
  Pallas kernels  165 us (99%)
    pallas_call x1, Pallas kernels, run_backward(): pl.pallas_call(functools.partial(backward_kernel, nz, items, orders, sche...  121 us
    pallas_call x1, Pallas kernels, run_forward(): pl.pallas_call(functools.partial(forward_kernel, nz), out_shape=[(pltpu.V...  33.7 us
    pallas_call x1, Pallas kernels, widen(): pl.pallas_call(kernel, out_shape=[jax.ShapeDtypeStruct(g.shape[::-1] if k...  10.4 us

profile of v1, /device:TPU:0, one launch (start us, length us, event | category | flops | bytes accessed | tf_op | source)
XLA Modules:
  0.0 166.6 jit_solution(4658328147977849081)
XLA Ops:
  0.6 33.7 %shard_map.254 = (bf16[128,768]{1,0:T(8,128)(2,1)S(1)}, bf16[1024,768]{1,0:T(8,128)(2,1)}, bf16[128,768]{1,0:T(8,128)(2,1)}, bf16[128,768]{1,0:T(8,128)(2,1)}, b...) custom-call(bf16[128,768]{1,0:T(8,128)(2,1)} %bitcast.4, ...), custom_call_target="tpu_custom_call" | custom-call | flops 1000000000 | bytes 20000000 | tf_op jit(solution)/shard_map/pallas_call | solution.py:604
  34.4 120.8 %shard_map.255 = (bf16[128,768]{1,0:T(8,128)(2,1)S(1)}, bf16[768,2304]{1,0:T(8,128)(2,1)S(1)}, bf16[768,768]{1,0:T(8,128)(2,1)S(1)}, bf16[3072,768]{1,0:T(8,128)...) custom-call(bf16[128,768]{1,0:T(8,128)(2,1)} %bitcast.5, bf16[128,768]{1,0:T(8,128)(2,1)} %bitcast.7, ...), custom_call_target="tpu_custom_call" | custom-call | tf_op jit(solution)/shard_map/pallas_call | solution.py:1104
  155.2 0.0 copy-start
  155.2 0.8 copy-done
  156.0 10.4 %shard_map.256 = (f32[768,2304]{1,0:T(8,128)}, f32[768,768]{1,0:T(8,128)}, f32[768,3072]{1,0:T(8,128)}, f32[3072,768]{1,0:T(8,128)}, f32[768]{0:T(1024)}, /*inde...) custom-call(bf16[768,2304]{1,0:T(8,128)(2,1)S(1)} %get-tuple-element, ...), custom_call_target="tpu_custom_call" | custom-call | tf_op jit(solution)/shard_map/pallas_call | solution.py:1207
Async XLA Ops:
  155.2 0.8 copy-start
